TPU v7x, 32 devices: a whole 2x2x4 slice. The times are simulated.
32 devices in a mesh: dp: 16 (over z, x, core), shard: 2 (over y).
Axes of the slice: x: 2, y: 2, z: 4, core: 2. Of those that a mesh axis runs over, the one named last changes fastest.
Arguments:
- clips: bfloat16 [64, 5, 256, 512], P(('dp', 'shard')), may hold values from -16 to 16
- code_grad: bfloat16 [64, 5, 256, 18], P(('dp', 'shard')), may hold values from -6 to 6
- conv_weight: bfloat16 [1536, 512], replicated, may hold values from -0.15625 to 0.15625
- norm_gain: float32 [512], replicated, may hold values from 0.5 to 1.5
- proj_weight: bfloat16 [512, 18], replicated, may hold values from -0.25 to 0.25
- code_bias: float32 [18], replicated, may hold values from -1 to 1
- rotation: float32 [18, 18], replicated, may hold values from -1.5 to 1.5
- first_moment: float32 [1536, 512], P('shard'), may hold values from -4 to 4
- second_moment: float32 [1536, 512], P('shard'), may hold values from 0.01 to 0.3
Outputs:
- new_weight: bfloat16 [1536, 512], replicated
- first_moment_out: float32 [1536, 512], P('shard')
- second_moment_out: float32 [1536, 512], P('shard')
- input_grad: bfloat16 [64, 5, 256, 512], P(('dp', 'shard'))
- loss: float32 [], replicated
All inputs are finite; a program needn't handle non-finite values.
Results may differ from a plain program's by a relative error of at most 0.014.
Values may be sent and summed in bfloat16 or wider, within the bound.
A program may use at most 128 MiB of HBM per device.

v0:
```python
import jax
import jax.numpy as jnp
from jax import lax
from jax.sharding import PartitionSpec as P


def stacked_taps(block):
    batch, frames, sites, width = block.shape
    padded = jnp.pad(block, ((0, 0), (2, 0), (0, 0), (0, 0)))
    taps = [padded[:, 2 - k : 2 - k + frames] for k in range(3)]
    return jnp.concatenate(taps, axis=3).reshape(batch * frames * sites, 3 * width)


def forward(block, conv_weight, norm_gain, proj_weight, code_bias, rotation):
    width = block.shape[3]
    stacked = stacked_taps(block)
    hidden = block.reshape(-1, width).astype(jnp.float32) + jnp.dot(
        stacked, conv_weight, preferred_element_type=jnp.float32
    )
    inverse = lax.rsqrt(jnp.mean(hidden * hidden, axis=1, keepdims=True) + 1e-06)
    unit = hidden * inverse
    normed = (unit * norm_gain).astype(jnp.bfloat16)
    latent = jnp.dot(normed, proj_weight, preferred_element_type=jnp.float32) + code_bias
    rotated = jnp.dot(latent, rotation, precision=lax.Precision.HIGHEST)
    codes = jnp.tanh(rotated)
    return (stacked, inverse, unit, rotated, codes)


def token_terms(rotated, codes, cotangent):
    probs = (1.0 + codes) / 2.0
    logit = 2.0 * rotated
    entropy = jax.nn.softplus(logit) - logit * probs
    token_loss = cotangent * codes + 0.25 * (rotated - codes) ** 2 + 0.1 * entropy
    return (probs, logit, jnp.sum(token_loss))


def backward(
    block, cotangent, conv_weight, norm_gain, proj_weight, rotation, saved, lean, clip_count
):
    stacked, inverse, unit, rotated, codes = saved
    probs = (1.0 + codes) / 2.0
    logit = 2.0 * rotated
    slope = 1.0 - codes * codes
    d_rot = (
        cotangent * slope
        + 0.5 * (rotated - codes) * (1.0 - slope)
        - 0.2 * logit * probs * (1.0 - probs)
        - 0.05 * slope * lean
    ) / clip_count
    d_lat = jnp.dot(d_rot, rotation.T, precision=lax.Precision.HIGHEST)
    d_norm = jnp.dot(d_lat, proj_weight.astype(jnp.float32).T, precision=lax.Precision.HIGHEST)
    scaled = d_norm * norm_gain
    d_hidden = inverse * (scaled - unit * jnp.mean(scaled * unit, axis=1, keepdims=True))
    d_conv = d_hidden.astype(jnp.bfloat16)
    batch, frames, sites, width = block.shape
    d_taps = lax.dot_general(
        d_conv, conv_weight, (((1,), (1,)), ((), ())), preferred_element_type=jnp.float32
    )
    d_taps = d_taps.reshape(batch, frames, sites, 3, width)
    padded = jnp.pad(d_taps, ((0, 0), (0, 2), (0, 0), (0, 0), (0, 0)))
    back = (
        padded[:, 0:frames, :, 0, :]
        + padded[:, 1 : frames + 1, :, 1, :]
        + padded[:, 2 : frames + 2, :, 2, :]
    )
    input_grad = (d_hidden.reshape(batch, frames, sites, width) + back).astype(jnp.bfloat16)
    return (stacked, d_conv, input_grad)


def on_device(
    clips,
    code_grad,
    conv_weight,
    norm_gain,
    proj_weight,
    code_bias,
    rotation,
    first_moment,
    second_moment,
):
    bit_count = code_grad.shape[3]
    devices = lax.axis_size("dp") * lax.axis_size("shard")
    clip_count = clips.shape[0] * devices
    token_count = clips.shape[0] * clips.shape[1] * clips.shape[2] * devices
    cotangent = code_grad.reshape(-1, bit_count).astype(jnp.float32)
    saved = forward(clips, conv_weight, norm_gain, proj_weight, code_bias, rotation)
    probs, logit, loss_part = token_terms(saved[3], saved[4], cotangent)
    bit_total, loss_total = lax.psum((jnp.sum(probs, axis=0), loss_part), ("dp", "shard"))
    bit_mean = bit_total / token_count
    code_entropy = jnp.sum(
        -bit_mean * jnp.log(bit_mean) - (1.0 - bit_mean) * jnp.log(1.0 - bit_mean)
    )
    loss = loss_total / token_count - 0.1 * code_entropy
    lean = jnp.log((1.0 - bit_mean) / bit_mean)
    stacked, d_conv, input_grad = backward(
        clips, cotangent, conv_weight, norm_gain, proj_weight, rotation, saved, lean, clip_count
    )
    owned_rows = first_moment.shape[0]
    whole_term = lax.dot_general(
        stacked, d_conv, (((0,), (0,)), ((), ())), preferred_element_type=jnp.float32
    )
    data_total = lax.psum(whole_term, "dp")
    grad_owned = lax.psum_scatter(
        data_total.astype(jnp.bfloat16), "shard", scatter_dimension=0, tiled=True
    ).astype(jnp.float32)
    first_out = 0.9 * first_moment + 0.1 * grad_owned
    second_out = 0.99 * second_moment + 0.01 * grad_owned * grad_owned
    owner = lax.axis_index("shard")
    own_weight = lax.dynamic_slice_in_dim(conv_weight, owner * owned_rows, owned_rows, 0).astype(
        jnp.float32
    )
    stepped = (own_weight - 0.001 * first_out / (jnp.sqrt(second_out) + 1e-08)).astype(jnp.bfloat16)
    new_weight = lax.all_gather(stepped, "shard", axis=0, tiled=True)
    return (new_weight, first_out, second_out, input_grad, loss)


def solution(mesh):
    return jax.shard_map(
        on_device,
        mesh=mesh,
        in_specs=(
            P(("dp", "shard"), None, None, None),
            P(("dp", "shard"), None, None, None),
            P(),
            P(),
            P(),
            P(),
            P(),
            P("shard", None),
            P("shard", None),
        ),
        out_specs=(
            P(),
            P("shard", None),
            P("shard", None),
            P(("dp", "shard"), None, None, None),
            P(),
        ),
        check_vma=False,
    )
```

profile of v0, /device:TPU:0, one launch (start us, length us, event | category | flops | bytes accessed | tf_op | source)
XLA Modules:
  0.0 240.6 jit_solution(17945013575079858273)
XLA Ops:
  7.2 0.0 copy-start
  7.2 0.0 copy-start.4
  7.2 0.0 reduce-scatter.2.cloned.1.call-start
  7.2 1.1 copy.18
  8.3 0.1 reshape.46
  8.4 2.5 %pad_slice_fusion.3 = (bf16[2,5,256,512]{3,2,1,0:T(8,128)(2,1)S(1)}, bf16[2,5,256,512]{3,2,1,0:T(8,128)(2,1)S(1)}) fusion(bf16[2,5,256,512]{3,2,1,0:T(8,128)(2,1)} %param.9), kind=kLoop, calls=%fused_computation.14 | loop fusion | bytes 7864320 | tf_op jit(solution)/shard_map/slice | solution.py:10
  10.9 0.0 copy-start.6
  10.9 0.8 pad_maximum_fusion
  11.8 0.6 copy-done.6
  12.3 4.7 %multiply_reduce_fusion.1 = (f32[2560]{0:T(1024)S(1)}, f32[2560,512]{1,0:T(8,128)S(1)}) fusion(bf16[2560,1536]{1,0:T(8,128)(2,1)S(1)} %bitcast.24, bf16[1536,512]{1,0:T(8,128)(2,1)S(1)} %copy-done.6, bf16[2560,512]{1,0:T(8,128)(2,1)S(1)} %bitcast.23), kind=kOutput, calls=%fused_computation.11 | convolution fusion | flops 4031772160 | bytes 17311744 | tf_op jit(solution)/shard_map/dot_general | solution.py:17
  17.1 0.0 copy-start.11
  17.1 2.3 copy-done.3
  19.4 1.0 convolution_add_fusion
  20.4 0.0 copy-done.11
  20.4 1.3 fusion.15
  21.7 42.4 %all-reduce.2 = (f32[18]{0:T(128)S(1)}, f32[]{:T(128)}) all-reduce(f32[18]{0:T(128)S(1)} %get-tuple-element.6, f32[]{:T(128)} %get-tuple-element.5), channel_id=1, replica_groups=mesh['dp'=16,'shard'=2] {'dp','shard'}, use_global_device_ids=true, to_apply=%region_2.3 | all-reduce | flops 19 | bytes 152 | tf_op jit(solution)/shard_map/psum | solution.py:88
  64.1 0.6 fusion.48
  64.7 0.5 fusion.22
  65.3 6.0 %multiply_reduce_fusion = (f32[2560]{0:T(1024)S(1)}, f32[2560,512]{1,0:T(8,128)S(1)}) fusion(f32[2560,512]{1,0:T(8,128)} %copy-done.3, f32[2560]{0:T(1024)S(1)} %add_rsqrt_fusion, f32[512]{0:T(512)S(1)} %copy-done.9, f32[2560,18]{0,1:T(8,128)S(1)} %fusion.22, bf16[512,18]{0,1:T(8,128)(2,1)S(1)} %copy-done), kind=kOutput, calls=%fused_computation.9 | convolution fusion | flops 288355840 | bytes 10711040 | tf_op jit(solution)/shard_map/dot_general | solution.py:51
  71.3 1.5 subtract_multiply_fusion
  72.9 2.3 copy-done.2
  75.1 6.0 %fusion.9 = f32[1536,512]{1,0:T(8,128)} fusion(bf16[2560,1536]{1,0:T(8,128)(2,1)S(1)} %bitcast.27, f32[2560,512]{1,0:T(8,128)S(1)} %subtract_multiply_fusion), kind=kOutput, calls=%fused_computation.25 | convolution fusion | flops 4027842560 | bytes 16252928 | tf_op jit(solution)/shard_map/dot_general | solution.py:99
  81.2 78.0 %all-reduce.4 = bf16[1536,512]{1,0:T(8,128)(2,1)} all-reduce(f32[1536,512]{1,0:T(8,128)} %fusion.9), channel_id=1, replica_groups=mesh['dp'=16,'shard'=2] {'dp'}, use_global_device_ids=true, to_apply=%region_4.5 | all-reduce | flops 786432 | bytes 4718592 | tf_op jit(solution)/shard_map/psum | solution.py:102
  159.2 0.0 reduce-scatter.2.cloned.1.call-update
  159.3 0.3 all-gather.2.cloned.1.call-start
  159.5 10.2 %fusion.7 = f32[2560,1536]{1,0:T(8,128)} fusion(bf16[1536,512]{1,0:T(8,128)(2,1)S(1)} %copy-done.7, f32[2560,512]{1,0:T(8,128)} %copy-done.2), kind=kOutput, calls=%fused_computation.23 | convolution fusion | flops 4027842560 | bytes 22544384 | tf_op jit(solution)/shard_map/dot_general | solution.py:56
  169.8 26.3 %reshape.44 = f32[2,5,256,3,512]{4,3,2,1,0:T(4,128)} reshape(f32[2560,1536]{1,0:T(8,128)} %fusion.7) | data formatting | bytes 31457280 | tf_op jit(solution)/shard_map/reshape | solution.py:59
  196.0 4.3 %subtract_convert_fusion = (bf16[768,512]{1,0:T(8,128)(2,1)}, f32[768,512]{1,0:T(8,128)}, f32[768,512]{1,0:T(8,128)}) fusion(bf16[1536,512]{1,0:T(8,128)(2,1)S(1)} %copy-done.7, s32[]{:T(128)S(6)} %select_n.7, bf16[768,512]{1,0:T(8,128)(2,1)} %reduce-scatter.2.cloned.1.call-done, f32[768,512]{1,0:T(8,128)S(1)} %copy-done.8, f32[768,512]{1,0:T(8,128)} %param.17), kind=kLoop, calls=%fused_computation.22 | loop fusion | flops 5505024 | bytes 8650756 | tf_op jit(solution)/shard_map/convert_element_type | solution.py:112
  200.3 0.0 all-gather.2.cloned.1.call-update
  200.4 21.8 %fusion.1 = f32[2,5,256,1,512]{4,3,2,1,0:T(1,128)} fusion(f32[2,5,256,3,512]{4,3,2,1,0:T(4,128)} %reshape.44), kind=kLoop, calls=%fused_computation.4 | loop fusion | flops 2621440 | bytes 31457280 | tf_op jit(solution)/shard_map/add | solution.py:62
  223.5 6.5 %fusion.2 = bf16[2,5,256,512]{3,2,1,0:T(8,128)(2,1)} fusion(f32[2,5,256,512]{3,2,1,0:T(8,128)} %bitcast.20, f32[2,5,256,1,512]{4,3,2,1,0:T(1,128)} %fusion.1), kind=kLoop, calls=%fused_computation.6 | loop fusion | flops 2621440 | bytes 13107200 | tf_op jit(solution)/shard_map/convert_element_type | solution.py:66
  230.0 2.7 %copy.24 = bf16[1536,512]{1,0:T(8,128)(2,1)} copy(bf16[1536,512]{1,0:T(8,128)(2,1)} %all-gather.2.cloned.1.call-done) | data formatting | bytes 3145728
  (30 shorter events, 0.1 us)
Async XLA Ops:
  7.2 12.2 %copy-start = (bf16[512,18]{0,1:T(8,128)(2,1)S(1)}, bf16[512,18]{0,1:T(8,128)(2,1)}, u32[]{:S(2)}) copy-start(bf16[512,18]{0,1:T(8,128)(2,1)} %param.13) | copy-start | bytes 55300
  7.2 3.7 %copy-start.4 = (bf16[2,5,256,512]{3,2,1,0:T(8,128)(2,1)S(1)}, bf16[2,5,256,512]{3,2,1,0:T(8,128)(2,1)}, u32[]{:S(2)}) copy-start(bf16[2,5,256,512]{3,2,1,0:T(8,128)(2,1)} %param.9) | copy-start | bytes 7864324
  7.2 188.8 %reduce-scatter.2.cloned.1.call-start = ((), (), s32[]{:S(2)}) async-start(), calls=%async_computation.1 | async-start | bytes 2359296 | tf_op jit(solution)/shard_map/reduce_scatter | solution.py:103
  10.9 1.4 copy-start.6
  11.8 5.3 %copy-start.5 = (bf16[2,5,256,1536]{3,2,1,0:T(8,128)(2,1)}, bf16[2,5,256,1536]{3,2,1,0:T(8,128)(2,1)S(1)}, u32[]{:S(2)}) copy-start(bf16[2,5,256,1536]{3,2,1,0:T(8,128)(2,1)S(1)} %pad_maximum_fusion) | copy-start | bytes 23592964
  12.3 7.1 %copy-start.9 = (f32[512]{0:T(512)S(1)}, f32[512]{0:T(512)}, u32[]{:S(2)}) copy-start(f32[512]{0:T(512)} %param.12) | copy-start | bytes 6148
  12.3 7.1 %copy-start.10 = (f32[18]{0:T(128)S(1)}, f32[18]{0:T(128)}, u32[]{:S(2)}) copy-start(f32[18]{0:T(128)} %param.14) | copy-start | bytes 220
  17.1 2.3 copy-start.3
  17.1 3.3 %copy-start.11 = (f32[18,18]{1,0:T(8,128)S(1)}, f32[18,18]{1,0:T(8,128)}, u32[]{:S(2)}) copy-start(f32[18,18]{1,0:T(8,128)} %param.15) | copy-start | bytes 3892
  64.7 6.6 %slice-start = ((s8[5242880]{0:T(1024)(128)(4,1)}), s8[4194304]{0:T(1024)(128)(4,1)S(1)}, s32[]{:S(2)}) async-start(s8[5242880]{0:T(1024)(128)(4,1)} %bitcast.21), calls=%async_computation.3 | async-start | bytes 8388608
  65.2 6.0 %slice-start.1 = ((s8[5242880]{0:T(1024)(128)(4,1)}), s8[1048576]{0:T(1024)(128)(4,1)S(1)}, s32[]{:S(2)}) async-start(s8[5242880]{0:T(1024)(128)(4,1)} %bitcast.21), calls=%async_computation.4 | async-start | bytes 2097152
  65.3 9.9 %slice-start.2 = ((s8[7864320]{0:T(1024)(128)(4,1)}), s8[4194304]{0:T(1024)(128)(4,1)S(1)}, s32[]{:S(2)}) async-start(s8[7864320]{0:T(1024)(128)(4,1)} %bitcast.25), calls=%async_computation.5 | async-start | bytes 8388608
  71.3 3.8 %slice-start.3 = ((s8[7864320]{0:T(1024)(128)(4,1)}), s8[3670016]{0:T(1024)(128)(4,1)S(1)}, s32[]{:S(2)}) async-start(s8[7864320]{0:T(1024)(128)(4,1)} %bitcast.25), calls=%async_computation.6 | async-start | bytes 7340032
  72.9 2.3 copy-start.2
  81.2 78.4 %copy-start.7 = (bf16[1536,512]{1,0:T(8,128)(2,1)S(1)}, bf16[1536,512]{1,0:T(8,128)(2,1)}, u32[]{:S(2)}) copy-start(bf16[1536,512]{1,0:T(8,128)(2,1)} %param.11) | copy-start | bytes 4718596
  159.3 70.7 %all-gather.2.cloned.1.call-start = ((), (), s32[]{:S(2)}) async-start(), calls=%async_computation.2 | async-start | bytes 2359296 | tf_op jit(solution)/shard_map/all_gather | solution.py:113
  169.8 26.3 %copy-start.8 = (f32[768,512]{1,0:T(8,128)S(1)}, f32[768,512]{1,0:T(8,128)}, u32[]{:S(2)}) copy-start(f32[768,512]{1,0:T(8,128)} %param.16) | copy-start | bytes 4718596
  223.5 9.1 %copy-start.1 = (bf16[512,18]{0,1:T(8,128)(2,1)S(1)}, bf16[512,18]{0,1:T(8,128)(2,1)}, u32[]{:S(2)}) copy-start(bf16[512,18]{0,1:T(8,128)(2,1)} %param.13) | copy-start | bytes 55300
Sparse Core Ops, SparseCore 0:
  159.4 24.4 reduce-scatter.1
  200.5 25.5 all-gather.1
where the time goes:
time: 242 us; the launch traced here: 241 us
  blocking collectives  120 us (50%)
  local copies, waits for them, and re-layouts  37.8 us (16%)
  other arithmetic  35.6 us (15%)
  matrix products  29.8 us (12%)
  between operations  16.7 us (7%)
    psum x1, blocking collectives, on_device(): data_total = lax.psum(whole_term, 'dp')  78 us
    psum x1, blocking collectives, on_device(): lax.psum((jnp.sum(probs, axis=0), loss_part), ('dp', 'shard'))  42.4 us
    reshape x1, local copies, waits for them, and re-layouts, backward(): d_taps = d_taps.reshape(batch, frames, sites, 3, width)  26.3 us
    add x1, other arithmetic, backward(): padded[:, 0:frames, :, 0, :] + padded[:, 1:frames + 1, :, 1, :]  21.8 us
    dot_general x1, matrix products, backward(): lax.dot_general(d_conv, conv_weight, (((1,), (1,)), ((), ())), preferred_...  10.2 us
    unnamed x33, local copies, waits for them, and re-layouts  7.84 us
    convert_element_type x1, other arithmetic, backward(): (d_hidden.reshape(batch, frames, sites, width) + back).astype(jnp.bfloat16)  6.48 us
    dot_general x1, matrix products, on_device(): lax.dot_general(stacked, d_conv, (((0,), (0,)), ((), ())), preferred_elem...  6.05 us
  transfers between devices with their start and end apart: 2, of which 0 were waited for; matrix products, arithmetic and copies ran while one was open for 27% of the time, Pallas kernels for 0%

commit v1 on v0

v1 whole, which is shorter than its diff:
```python
import functools

import jax
import jax.numpy as jnp
from jax import lax
from jax.experimental import pallas as pl
from jax.experimental.pallas import tpu as pltpu
from jax.sharding import PartitionSpec as P

MESH = pl.DeviceIdType.MESH
F32 = jnp.float32
BF16 = jnp.bfloat16
HIGHEST = lax.Precision.HIGHEST
BITS_PAD = 32
PLANE = 8
LINE = 4
DEPTH = 16

IN_W, IN_CG, IN_M1, IN_M2, OUT_W, OUT_M1, OUT_M2, IN_X = range(8)
(
    T_PLANE,
    T_LINE,
    T_CORE,
    T_FIRST,
    T_SECOND,
    T_ROWS,
    T_GATHER,
    T_GRAD_X,
    T_GRAD_CORE,
    T_NEW_Y,
    T_NEW_CORE,
    T_FAR,
) = (0, 8, 12, 14, 16, 17, 21, 25, 26, 28, 30, 32)

NN = (((1,), (0,)), ((), ()))
NT = (((1,), (1,)), ((), ()))


def dot(a, b, dims=NN, precision=None):
    return lax.dot_general(a, b, dims, precision=precision, preferred_element_type=F32)


def flip(bit, change):
    return bit + (1 - 2 * bit) if change else bit


def kernel(
    sizes,
    clips_hbm,
    cg_hbm,
    weight_hbm,
    gain_ref,
    proj_ref,
    bias_ref,
    rot_ref,
    m1_hbm,
    m2_hbm,
    nw_hbm,
    m1o_hbm,
    m2o_hbm,
    ig_hbm,
    loss_ref,
    xs,
    xt,
    w,
    wt,
    cg,
    unit,
    inv,
    rott,
    cgt,
    dl,
    pp,
    dh,
    dc,
    ig,
    m1,
    m2,
    g,
    r1,
    keep,
    s2,
    r2,
    s3,
    r3,
    s4,
    r4,
    far,
    gr,
    nw,
    stat,
    stat2,
    stat3,
    local_sem,
    send_sem,
    recv_sem,
):
    clips, frames, sites, width, bits, dp_size, far_size, tokens_all, clips_all = sizes
    clip_rows = frames * sites
    half = m1.shape[0]
    per_core, per_x = half // 2, half // 4
    own = half // DEPTH
    dp = lax.axis_index("dp")
    s = lax.axis_index("shard")
    c = dp % 2
    h = (dp // 2) % 2
    z = (dp // 4) % 4
    z0, z1 = z % 2, z // 2
    f = dp // DEPTH

    def plane_peer(r):
        return (dp - c - 2 * h + flip(c, r & 1) + 2 * flip(h, r & 2), flip(s, r & 4))

    def line_at(r):
        return flip(z0, r & 1) + 2 * flip(z1, r & 2)

    def line_peer(r):
        return (dp + 4 * (line_at(r) - z), s)

    def far_at(r):
        return (f + r) % far_size

    def far_peer(r):
        return (dp + DEPTH * (far_at(r) - f), s)

    def send(src, dst, index, peer):
        copy = pltpu.make_async_remote_copy(
            src_ref=src,
            dst_ref=dst,
            send_sem=send_sem.at[index],
            recv_sem=recv_sem.at[index],
            device_id=peer,
            device_id_type=MESH,
        )
        copy.start()
        return copy

    w_in = pltpu.make_async_copy(weight_hbm, w, local_sem.at[IN_W])
    w_in.start()
    x_in = []
    for clip in range(clips):
        rows = pl.ds(clip * clip_rows, clip_rows)
        copy = pltpu.make_async_copy(clips_hbm.at[rows], xs.at[rows], local_sem.at[IN_X + clip])
        copy.start()
        x_in.append(copy)
    cg_in = pltpu.make_async_copy(cg_hbm, cg, local_sem.at[IN_CG])
    cg_in.start()
    m1_in = pltpu.make_async_copy(m1_hbm, m1, local_sem.at[IN_M1])
    m1_in.start()
    m2_in = pltpu.make_async_copy(m2_hbm, m2, local_sem.at[IN_M2])
    m2_in.start()

    barrier = pltpu.get_barrier_semaphore()
    peers = [plane_peer(r) for r in range(1, PLANE)]
    peers += [line_peer(r) for r in range(1, LINE)]
    for r in range(1, far_size):
        peers.append(far_peer(r))
    for peer in peers:
        pl.semaphore_signal(barrier, inc=1, device_id=peer, device_id_type=MESH)

    eye_mask = lax.broadcasted_iota(jnp.int32, (BITS_PAD, bits), 0) == lax.broadcasted_iota(
        jnp.int32, (BITS_PAD, bits), 1
    )
    eye = jnp.where(eye_mask, 1.0, 0.0).astype(F32)
    eye16 = eye.astype(BF16)
    proj_t = dot(eye16, proj_ref[...], NT).astype(BF16)
    pp[...] = jnp.zeros_like(pp)
    pp[0:BITS_PAD, :] = proj_t
    pp[BITS_PAD : 2 * BITS_PAD, :] = proj_t
    dl[...] = jnp.zeros_like(dl)
    rot_rows = dot(eye, rot_ref[...], NN, HIGHEST)
    rot = dot(rot_rows, eye, NT, HIGHEST)
    rot_t = dot(eye, rot_rows, NT, HIGHEST)
    bias = jnp.sum(jnp.where(eye_mask, bias_ref[...], 0.0), axis=1, keepdims=True)
    gain = gain_ref[...]

    w_in.wait()
    for copy in x_in:
        copy.wait()
    cg_in.wait()

    def forward(clip, carry):
        base = pl.multiple_of(clip * clip_rows, clip_rows)
        for frame in range(frames):
            here = pl.ds(pl.multiple_of(base + frame * sites, sites), sites)
            taps = min(frame, 2) + 1
            parts = [
                xs[pl.ds(pl.multiple_of(base + (frame - k) * sites, sites), sites), :]
                for k in range(taps)
            ]
            lhs = parts[0] if taps == 1 else jnp.concatenate(parts, axis=1)
            hidden = parts[0].astype(F32) + dot(lhs, w[0 : taps * width, :])
            scale = lax.rsqrt(jnp.mean(hidden * hidden, axis=1, keepdims=True) + 1e-06)
            u = hidden * scale
            unit[here, :] = u
            inv[here, :] = scale
            normed = (u * gain).astype(BF16)
            lat = dot(proj_t, normed, NT) + bias
            rott[:, here] = dot(rot_t, lat, NN, HIGHEST)
            cgt[:, here] = dot(eye16, cg[here, :], NT)
        return carry

    lax.fori_loop(0, clips, forward, 0)

    rotated = rott[...]
    cotangent = cgt[...]
    codes = jnp.tanh(rotated)
    probs = (1.0 + codes) / 2.0
    logit = 2.0 * rotated
    softplus = jnp.maximum(logit, 0.0) + jnp.log(1.0 + jnp.exp(-jnp.abs(logit)))
    entropy = softplus - logit * probs
    token_loss = cotangent * codes + 0.25 * (rotated - codes) ** 2 + 0.1 * entropy
    real = lax.broadcasted_iota(jnp.int32, (BITS_PAD, 1), 0) < bits
    loss_part = jnp.sum(
        jnp.where(real, jnp.sum(token_loss, axis=1, keepdims=True), 0.0), axis=0, keepdims=True
    )
    bit_part = jnp.sum(probs, axis=1, keepdims=True)
    column = jnp.where(real, bit_part, loss_part)
    stat[0] = jnp.broadcast_to(column, stat.shape[1:])

    pl.semaphore_wait(barrier, len(peers))
    sent = [send(stat.at[0], stat.at[r], T_PLANE + r, plane_peer(r)) for r in range(1, PLANE)]

    for k in range(3):
        wt[k * width : (k + 1) * width, :] = w[k * width : (k + 1) * width, :].T
    for copy in sent:
        copy.wait()
    total = stat[0]
    for r in range(1, PLANE):
        total = total + stat[r]
    stat2[0] = total
    sent = [send(stat2.at[0], stat2.at[r], T_LINE + r, line_peer(r)) for r in range(1, LINE)]

    def turn(clip, carry):
        base = pl.multiple_of(clip * clip_rows, clip_rows)
        for frame in range(frames):
            here = pl.ds(pl.multiple_of(base + frame * sites, sites), sites)
            xt[:, here] = xs[here, :].T
        return carry

    lax.fori_loop(0, clips, turn, 0)
    for copy in sent:
        copy.wait()
    total = stat2[0]
    for r in range(1, LINE):
        total = total + stat2[r]
    if far_size > 1:
        stat3[f] = total
        sent = [
            send(stat3.at[f], stat3.at[f], T_FAR + r, far_peer(r)) for r in range(1, far_size)
        ]
        for copy in sent:
            copy.wait()
        total = stat3[0]
        for r in range(1, far_size):
            total = total + stat3[r]
    total = total[:, 0:1]
    bit_mean = jnp.where(real, total / tokens_all, 0.5)
    code_entropy = -bit_mean * jnp.log(bit_mean) - (1.0 - bit_mean) * jnp.log(1.0 - bit_mean)
    code_entropy = jnp.sum(jnp.where(real, code_entropy, 0.0), axis=0, keepdims=True)
    loss_ref[...] = total[bits : bits + 1, :] / tokens_all - 0.1 * code_entropy
    lean = jnp.log((1.0 - bit_mean) / bit_mean)

    rotated = rott[...]
    codes = jnp.tanh(rotated)
    probs = (1.0 + codes) / 2.0
    logit = 2.0 * rotated
    slope = 1.0 - codes * codes
    d_rot = (
        cgt[...] * slope
        + 0.5 * (rotated - codes) * (1.0 - slope)
        - 0.2 * logit * probs * (1.0 - probs)
        - 0.05 * slope * lean
    ) / clips_all
    d_lat = dot(rot, d_rot, NN, HIGHEST)
    high = d_lat.astype(BF16)
    dl[0:BITS_PAD, :] = high.astype(F32)
    dl[BITS_PAD : 2 * BITS_PAD, :] = d_lat - high.astype(F32)

    def back(clip, carry):
        base = pl.multiple_of(clip * clip_rows, clip_rows)
        for frame in range(frames):
            here = pl.ds(pl.multiple_of(base + frame * sites, sites), sites)
            a = dot(dl[:, here].T.astype(BF16), pp[...]) * gain
            u = unit[here, :]
            d_hidden = inv[here, :] * (a - u * jnp.mean(a * u, axis=1, keepdims=True))
            dh[here, :] = d_hidden
            dc[here, :] = d_hidden.astype(BF16)
        return carry

    lax.fori_loop(0, clips, back, 0)

    core_peer = plane_peer(1)
    core_sent = []
    for k in range(3):
        term = None
        for clip in range(clips):
            start = clip * clip_rows
            depth = (frames - k) * sites
            part = dot(
                xt[:, start : start + depth],
                dc[start + k * sites : start + clip_rows, :],
            )
            term = part if term is None else term + part
        g[k * width : (k + 1) * width, :] = term
        for j in range(2):
            if (k + 1) * width >= (j + 1) * half > k * width:
                rows = pl.ds(pl.multiple_of(j * half + (1 - c) * per_core, 8), per_core)
                core_sent.append(send(g.at[rows], r1.at[j], T_CORE + j, core_peer))

    def input_grad(clip):
        base = clip * clip_rows
        for frame in range(frames):
            here = pl.ds(base + frame * sites, sites)
            taps = min(frames - 1 - frame, 2) + 1
            parts = [dc[pl.ds(base + (frame + k) * sites, sites), :] for k in range(taps)]
            lhs = parts[0] if taps == 1 else jnp.concatenate(parts, axis=1)
            ig[here, :] = (dh[here, :] + dot(lhs, wt[0 : taps * width, :])).astype(BF16)
        rows = pl.ds(base, clip_rows)
        copy = pltpu.make_async_copy(ig.at[rows], ig_hbm.at[rows], local_sem.at[IN_X + clips + clip])
        copy.start()
        return copy

    ig_out = []
    for copy in core_sent:
        copy.wait()

    first_peer = (dp + (1 - c) * 2 * (1 - 2 * h), s + c * (1 - 2 * s))
    second_peer = (dp + c * 2 * (1 - 2 * h), s + (1 - c) * (1 - 2 * s))

    def summed(side, x):
        rows = pl.ds(pl.multiple_of(side * half + c * per_core + x * per_x, 8), per_x)
        return g[rows, :] + r1[side, pl.ds(pl.multiple_of(x * per_x, 8), per_x), :]

    first_sent = []
    for j in range(2):
        s2[j] = summed((1 - c) * j + c * (1 - s), (1 - c) * (1 - h) + c * j).astype(BF16)
        first_sent.append(send(s2.at[j], r2.at[j], T_FIRST + j, first_peer))
    for j in range(2):
        keep[j] = summed((1 - c) * j + c * s, (1 - c) * h + c * j)
    ig_out.append(input_grad(0))
    for copy in first_sent:
        copy.wait()
    kept = (1 - c) * s + c * h
    s3[...] = (keep[1 - kept] + r2[1 - kept].astype(F32)).astype(BF16)
    second_sent = send(s3, r3, T_SECOND, second_peer)
    keep[kept] = keep[kept] + r2[kept].astype(F32)
    m1_in.wait()
    m2_in.wait()
    second_sent.wait()
    mine = keep[kept] + r3[...].astype(F32)
    s4[...] = mine.astype(BF16)
    keep[kept] = mine
    rows_sent = []
    for r in range(1, LINE):
        rows = pl.ds(pl.multiple_of(line_at(r) * own, 16), own)
        rows_sent.append(send(s4.at[rows], r4.at[r], T_ROWS + r, line_peer(r)))
    for clip in range(1, clips):
        ig_out.append(input_grad(clip))
    for copy in rows_sent:
        copy.wait()
    grad = keep[kept, pl.ds(pl.multiple_of(z * own, 8), own), :]
    for r in range(1, LINE):
        grad = grad + r4[r].astype(F32)
    if far_size > 1:
        far[f] = grad
        sent = [
            send(far.at[f], far.at[f], T_FAR + far_size + r, far_peer(r))
            for r in range(1, far_size)
        ]
        for copy in sent:
            copy.wait()
        grad = far[0]
        for r in range(1, far_size):
            grad = grad + far[r]

    mine_at = c * per_core + h * per_x
    own_rows = pl.ds(pl.multiple_of(mine_at + z * own, 16), own)
    gr[own_rows, :] = grad.astype(BF16)
    sent = [
        send(gr.at[own_rows], gr.at[own_rows], T_GATHER + r, line_peer(r)) for r in range(1, LINE)
    ]
    for copy in sent:
        copy.wait()

    def update(at):
        rows = pl.ds(pl.multiple_of(at, 16), per_x)
        here = pl.ds(pl.multiple_of(s * half + at, 16), per_x)
        value = gr[rows, :].astype(F32)
        first = 0.9 * m1[rows, :] + 0.1 * value
        second = 0.99 * m2[rows, :] + 0.01 * value * value
        m1[rows, :] = first
        m2[rows, :] = second
        stepped = w[here, :].astype(F32) - 0.001 * first / (jnp.sqrt(second) + 1e-08)
        nw[here, :] = stepped.astype(BF16)

    def grad_rows(at):
        return gr.at[pl.ds(pl.multiple_of(at, 16), per_x)]

    def new_rows(side, at):
        return nw.at[pl.ds(pl.multiple_of(side * half + at, 16), per_x)]

    x_peer, y_peer = plane_peer(2), plane_peer(4)
    other_at = c * per_core + (1 - h) * per_x
    grad_x = send(grad_rows(mine_at), grad_rows(mine_at), T_GRAD_X, x_peer)
    grad_core = [send(grad_rows(mine_at), grad_rows(mine_at), T_GRAD_CORE, core_peer)]
    update(mine_at)
    new_y = [send(new_rows(s, mine_at), new_rows(s, mine_at), T_NEW_Y, y_peer)]
    grad_x.wait()
    grad_core.append(send(grad_rows(other_at), grad_rows(other_at), T_GRAD_CORE + 1, core_peer))
    update(other_at)
    new_y.append(send(new_rows(s, other_at), new_rows(s, other_at), T_NEW_Y + 1, y_peer))
    grad_core[0].wait()
    update((1 - c) * per_core + h * per_x)
    grad_core[1].wait()
    update((1 - c) * per_core + (1 - h) * per_x)
    m1_out = pltpu.make_async_copy(m1, m1o_hbm, local_sem.at[OUT_M1])
    m1_out.start()
    m2_out = pltpu.make_async_copy(m2, m2o_hbm, local_sem.at[OUT_M2])
    m2_out.start()
    new_core = []
    for j, at in enumerate((mine_at, other_at)):
        new_y[j].wait()
        new_core.append(send(new_rows(1 - s, at), new_rows(1 - s, at), T_NEW_CORE + j, core_peer))
    for copy in new_core:
        copy.wait()
    nw_out = pltpu.make_async_copy(nw, nw_hbm, local_sem.at[OUT_W])
    nw_out.start()
    for copy in ig_out:
        copy.wait()
    m1_out.wait()
    m2_out.wait()
    nw_out.wait()


def on_device(
    clips,
    code_grad,
    conv_weight,
    norm_gain,
    proj_weight,
    code_bias,
    rotation,
    first_moment,
    second_moment,
):
    count, frames, sites, width = clips.shape
    bits = code_grad.shape[3]
    dp_size = lax.axis_size("dp")
    devices = dp_size * lax.axis_size("shard")
    far_size = dp_size // DEPTH
    tokens = count * frames * sites
    rows, half = conv_weight.shape[0], first_moment.shape[0]
    per_core, per_x, own = half // 2, half // 4, half // DEPTH
    sizes = (
        count,
        frames,
        sites,
        width,
        bits,
        dp_size,
        far_size,
        tokens * devices,
        count * devices,
    )
    vmem = pltpu.VMEM
    scratch = [
        vmem((tokens, width), BF16),
        vmem((width, tokens), BF16),
        vmem((rows, width), BF16),
        vmem((rows, width), BF16),
        vmem((tokens, bits), BF16),
        vmem((tokens, width), F32),
        vmem((tokens, 1), F32),
        vmem((BITS_PAD, tokens), F32),
        vmem((BITS_PAD, tokens), F32),
        vmem((128, tokens), F32),
        vmem((128, width), BF16),
        vmem((tokens, width), F32),
        vmem((tokens, width), BF16),
        vmem((tokens, width), BF16),
        vmem((half, width), F32),
        vmem((half, width), F32),
        vmem((rows, width), F32),
        vmem((2, per_core, width), F32),
        vmem((2, per_x, width), F32),
        vmem((2, per_x, width), BF16),
        vmem((2, per_x, width), BF16),
        vmem((per_x, width), BF16),
        vmem((per_x, width), BF16),
        vmem((per_x, width), BF16),
        vmem((LINE, own, width), BF16),
        vmem((far_size, own, width), F32),
        vmem((half, width), BF16),
        vmem((rows, width), BF16),
        vmem((PLANE, BITS_PAD, 128), F32),
        vmem((LINE, BITS_PAD, 128), F32),
        vmem((far_size, BITS_PAD, 128), F32),
        pltpu.SemaphoreType.DMA((IN_X + 2 * count,)),
        pltpu.SemaphoreType.DMA((T_FAR + 2 * far_size,)),
        pltpu.SemaphoreType.DMA((T_FAR + 2 * far_size,)),
    ]
    whole = pl.BlockSpec(memory_space=pltpu.VMEM)
    outside = pl.BlockSpec(memory_space=pl.ANY)
    new_weight, first_out, second_out, input_grad, loss = pl.pallas_call(
        functools.partial(kernel, sizes),
        out_shape=(
            jax.ShapeDtypeStruct((rows, width), BF16),
            jax.ShapeDtypeStruct((half, width), F32),
            jax.ShapeDtypeStruct((half, width), F32),
            jax.ShapeDtypeStruct((tokens, width), BF16),
            jax.ShapeDtypeStruct((1, 1), F32),
        ),
        in_specs=[outside, outside, outside, whole, whole, whole, whole, outside, outside],
        out_specs=(outside, outside, outside, outside, whole),
        scratch_shapes=scratch,
        compiler_params=pltpu.CompilerParams(
            collective_id=0, has_side_effects=True, vmem_limit_bytes=60 * 1024 * 1024
        ),
    )(
        clips.reshape(tokens, width),
        code_grad.reshape(tokens, bits),
        conv_weight,
        norm_gain.reshape(1, width),
        proj_weight,
        code_bias.reshape(1, bits),
        rotation,
        first_moment,
        second_moment,
    )
    return (
        new_weight,
        first_out,
        second_out,
        input_grad.reshape(clips.shape),
        loss.reshape(()),
    )


def solution(mesh):
    return jax.shard_map(
        on_device,
        mesh=mesh,
        in_specs=(
            P(("dp", "shard"), None, None, None),
            P(("dp", "shard"), None, None, None),
            P(),
            P(),
            P(),
            P(),
            P(),
            P("shard", None),
            P("shard", None),
        ),
        out_specs=(
            P(),
            P("shard", None),
            P("shard", None),
            P(("dp", "shard"), None, None, None),
            P(),
        ),
        check_vma=False,
    )
```

time: 242 us -> 82.2 us (0.34)
  blocking collectives: 120 us -> 0 us
  Pallas kernels: 0 us -> 67.3 us
  other arithmetic: 35.6 us -> 0 us
  matrix products: 29.8 us -> 0 us
  local copies, waits for them, and re-layouts: 37.8 us -> 12.1 us
  between operations: 16.7 us -> 2.42 us
    psum x2 -> x0, blocking collectives: 120 us -> none  [the longest x1 78 us: on_device(): data_total = lax.psum(whole_term, 'dp')]
    pallas_call x0 -> x1, Pallas kernels: none -> 67.3 us  [on_device(): pl.pallas_call(functools.partial(kernel, sizes), out_shape=(jax.ShapeDtyp...]
    dot_general x7 -> x0, matrix products: 29.8 us -> none  [the longest x1 10.2 us: backward(): lax.dot_general(d_conv, conv_weight, (((1,), (1,)), ((), ())), preferred_...]
    reshape x1 -> x0, local copies, waits for them, and re-layouts: 26.3 us -> none  [backward(): d_taps = d_taps.reshape(batch, frames, sites, 3, width)]
    add x1 -> x0, other arithmetic: 21.8 us -> none  [backward(): padded[:, 0:frames, :, 0, :] + padded[:, 1:frames + 1, :, 1, :]]
    convert_element_type x2 -> x0, other arithmetic: 10.8 us -> none  [the longest x1 6.48 us: backward(): (d_hidden.reshape(batch, frames, sites, width) + back).astype(jnp.bfloat16)]
    unnamed x33 -> x12, local copies, waits for them, and re-layouts: 7.84 us -> 12.1 us
    slice x1 -> x0, local copies, waits for them, and re-layouts: 2.52 us -> none  [stacked_taps(): taps = [padded[:, 2 - k:2 - k + frames] for k in range(3)]]
  transfers between devices with their start and end apart: 2 -> 0, of which waited for: 0 -> 0; matrix products, arithmetic and copies ran while one was open for 27% -> 0% of each run, Pallas kernels for 0% -> 0%
where the time goes in v1:
time: 82.2 us; the launch traced here: 81.8 us
  Pallas kernels  67.3 us (82%)
  local copies, waits for them, and re-layouts  12.1 us (15%)
  between operations  2.42 us (3%)
    pallas_call x1, Pallas kernels, on_device(): pl.pallas_call(functools.partial(kernel, sizes), out_shape=(jax.ShapeDtyp...  67.3 us
    unnamed x12, local copies, waits for them, and re-layouts  12.1 us

profile of v1, /device:TPU:0, one launch (start us, length us, event | category | flops | bytes accessed | tf_op | source)
XLA Modules:
  0.0 81.8 jit_solution(4629309516798054982)
XLA Ops:
  0.6 1.5 %copy.15.proj_ref = bf16[512,18]{1,0:T(8,128)(2,1)} copy(bf16[512,18]{0,1:T(8,128)(2,1)} %param.13) | data formatting | bytes 36864 | tf_op args[4]
  2.2 2.0 %copy.14 = bf16[2,5,256,18]{3,2,1,0:T(8,128)(2,1)} copy(bf16[2,5,256,18]{2,0,3,1:T(2,128)(2,1)} %param.10) | data formatting | bytes 184320 | tf_op args[1]
  4.2 67.3 %shard_map.128 = (bf16[1536,512]{1,0:T(8,128)(2,1)}, f32[768,512]{1,0:T(8,128)}, f32[768,512]{1,0:T(8,128)}, bf16[2560,512]{1,0:T(8,128)(2,1)}, f32[1,1]{1,0:T(1,128)}) custom-call(bf16[2560,512]{1,0:T(8,128)(2,1)} %bitcast.7, bf16[2560,18]{1,0:T(8,128)(2,1)} %bitcast.6, bf16[1536,512]{1,0:T(8,128)(2,1)} %weight_hbm.1, f32[1,512]{1,0:T(1,128)} %bitcast.9, ...), custom_call_target="tpu_custom_call" | custom-call | tf_op jit(solution)/shard_map/pallas_call | solution.py:505
  71.5 0.0 copy-start.2
  71.5 2.8 %copy.21 = bf16[1536,512]{1,0:T(8,128)(2,1)} copy(bf16[1536,512]{1,0:T(8,128)(2,1)} %get-tuple-element.20) | data formatting | bytes 3145728
  74.3 0.0 copy-done.2
  74.3 0.0 copy-start.1
  74.3 1.1 %copy.22 = f32[768,512]{1,0:T(8,128)} copy(f32[768,512]{1,0:T(8,128)S(1)} %copy-done.2) | data formatting | bytes 3145728
  75.4 0.8 %copy-done.1 = f32[768,512]{1,0:T(8,128)S(1)} copy-done((f32[768,512]{1,0:T(8,128)S(1)}, f32[768,512]{1,0:T(8,128)}, u32[]{:S(2)}) %copy-start.1) | copy-done | bytes 1572888
  76.3 0.0 copy-start
  76.3 1.1 %copy.23 = f32[768,512]{1,0:T(8,128)} copy(f32[768,512]{1,0:T(8,128)S(1)} %copy-done.1) | data formatting | bytes 3145728
  77.4 1.2 %copy-done = bf16[2560,512]{1,0:T(8,128)(2,1)S(1)} copy-done((bf16[2560,512]{1,0:T(8,128)(2,1)S(1)}, bf16[2560,512]{1,0:T(8,128)(2,1)}, u32[]{:S(2)}) %copy-start) | copy-done | bytes 2621464
  78.6 1.5 %copy.24 = bf16[2,5,256,512]{3,2,1,0:T(8,128)(2,1)} copy(bf16[2,5,256,512]{3,2,1,0:T(8,128)(2,1)S(1)} %bitcast.8) | data formatting | bytes 5242880
Async XLA Ops:
  71.5 2.8 %copy-start.2 = (f32[768,512]{1,0:T(8,128)S(1)}, f32[768,512]{1,0:T(8,128)}, u32[]{:S(2)}) copy-start(f32[768,512]{1,0:T(8,128)} %get-tuple-element.21) | copy-start | bytes 4718596
  74.3 2.0 %copy-start.1 = (f32[768,512]{1,0:T(8,128)S(1)}, f32[768,512]{1,0:T(8,128)}, u32[]{:S(2)}) copy-start(f32[768,512]{1,0:T(8,128)} %get-tuple-element.22) | copy-start | bytes 4718596
  76.3 2.3 %copy-start = (bf16[2560,512]{1,0:T(8,128)(2,1)S(1)}, bf16[2560,512]{1,0:T(8,128)(2,1)}, u32[]{:S(2)}) copy-start(bf16[2560,512]{1,0:T(8,128)(2,1)} %get-tuple-element.13) | copy-start | bytes 7864324

commit v2 on v1

--- a/solution.py
+++ b/solution.py
@@ -15,6 +15,8 @@
 PLANE = 8
 LINE = 4
 DEPTH = 16
+PIECES = 2
+VMEM_BYTES = 60 * 1024 * 1024
 
 IN_W, IN_CG, IN_M1, IN_M2, OUT_W, OUT_M1, OUT_M2, IN_X = range(8)
 (
@@ -28,9 +30,10 @@
     T_GRAD_X,
     T_GRAD_CORE,
     T_NEW_Y,
+    T_NEW_X,
     T_NEW_CORE,
     T_FAR,
-) = (0, 8, 12, 14, 16, 17, 21, 25, 26, 28, 30, 32)
+) = (0, 8, 12, 14, 16, 17, 21, 25, 29, 37, 45, 47, 55)
 
 NN = (((1,), (0,)), ((), ()))
 NT = (((1,), (1,)), ((), ()))
@@ -67,11 +70,11 @@
     cg,
     unit,
     inv,
+    lat,
     rott,
     cgt,
     dl,
     pp,
-    dh,
     dc,
     ig,
     m1,
@@ -97,6 +100,7 @@
 ):
     clips, frames, sites, width, bits, dp_size, far_size, tokens_all, clips_all = sizes
     clip_rows = frames * sites
+    block = clips * sites
     half = m1.shape[0]
     per_core, per_x = half // 2, half // 4
     own = half // DEPTH
@@ -138,11 +142,15 @@
     w_in = pltpu.make_async_copy(weight_hbm, w, local_sem.at[IN_W])
     w_in.start()
     x_in = []
-    for clip in range(clips):
-        rows = pl.ds(clip * clip_rows, clip_rows)
-        copy = pltpu.make_async_copy(clips_hbm.at[rows], xs.at[rows], local_sem.at[IN_X + clip])
-        copy.start()
-        x_in.append(copy)
+    for frame in range(frames):
+        for clip in range(clips):
+            copy = pltpu.make_async_copy(
+                clips_hbm.at[pl.ds(clip * clip_rows + frame * sites, sites)],
+                xs.at[pl.ds(frame * block + clip * sites, sites)],
+                local_sem.at[IN_X + frame * clips + clip],
+            )
+            copy.start()
+            x_in.append(copy)
     cg_in = pltpu.make_async_copy(cg_hbm, cg, local_sem.at[IN_CG])
     cg_in.start()
     m1_in = pltpu.make_async_copy(m1_hbm, m1, local_sem.at[IN_M1])
@@ -163,7 +171,7 @@
     )
     eye = jnp.where(eye_mask, 1.0, 0.0).astype(F32)
     eye16 = eye.astype(BF16)
-    proj_t = dot(eye16, proj_ref[...], NT).astype(BF16)
+    proj_t = dot(eye16, proj_ref[...]).astype(BF16)
     pp[...] = jnp.zeros_like(pp)
     pp[0:BITS_PAD, :] = proj_t
     pp[BITS_PAD : 2 * BITS_PAD, :] = proj_t
@@ -175,33 +183,30 @@
     gain = gain_ref[...]
 
     w_in.wait()
-    for copy in x_in:
-        copy.wait()
+
+    for frame in range(frames):
+        here = slice(frame * block, (frame + 1) * block)
+        for copy in x_in[frame * clips : (frame + 1) * clips]:
+            copy.wait()
+        taps = min(frame, 2) + 1
+        parts = [xs[(frame - k) * block : (frame - k + 1) * block, :] for k in range(taps)]
+        lhs = parts[0] if taps == 1 else jnp.concatenate(parts, axis=1)
+        hidden = parts[0].astype(F32) + dot(lhs, w[0 : taps * width, :])
+        scale = lax.rsqrt(jnp.mean(hidden * hidden, axis=1, keepdims=True) + 1e-06)
+        u = hidden * scale
+        unit[here, :] = u
+        inv[here, :] = scale
+        normed = (u * gain).astype(BF16)
+        lat[:, here] = dot(proj_t, normed, NT) + bias
+
+    rott[...] = dot(rot_t, lat[...], NN, HIGHEST)
     cg_in.wait()
-
-    def forward(clip, carry):
-        base = pl.multiple_of(clip * clip_rows, clip_rows)
-        for frame in range(frames):
-            here = pl.ds(pl.multiple_of(base + frame * sites, sites), sites)
-            taps = min(frame, 2) + 1
-            parts = [
-                xs[pl.ds(pl.multiple_of(base + (frame - k) * sites, sites), sites), :]
-                for k in range(taps)
-            ]
-            lhs = parts[0] if taps == 1 else jnp.concatenate(parts, axis=1)
-            hidden = parts[0].astype(F32) + dot(lhs, w[0 : taps * width, :])
-            scale = lax.rsqrt(jnp.mean(hidden * hidden, axis=1, keepdims=True) + 1e-06)
-            u = hidden * scale
-            unit[here, :] = u
-            inv[here, :] = scale
-            normed = (u * gain).astype(BF16)
-            lat = dot(proj_t, normed, NT) + bias
-            rott[:, here] = dot(rot_t, lat, NN, HIGHEST)
-            cgt[:, here] = dot(eye16, cg[here, :], NT)
-        return carry
-
-    lax.fori_loop(0, clips, forward, 0)
-
+    cgt[...] = jnp.zeros_like(cgt)
+    for frame in range(frames):
+        value = cg[frame].astype(F32)
+        for clip in range(clips):
+            start = frame * block + clip * sites
+            cgt[0:bits, start : start + sites] = value[:, clip, :]
     rotated = rott[...]
     cotangent = cgt[...]
     codes = jnp.tanh(rotated)
@@ -221,6 +226,14 @@
     pl.semaphore_wait(barrier, len(peers))
     sent = [send(stat.at[0], stat.at[r], T_PLANE + r, plane_peer(r)) for r in range(1, PLANE)]
 
+    slope = 1.0 - codes * codes
+    base = (
+        cotangent * slope
+        + 0.5 * (rotated - codes) * (1.0 - slope)
+        - 0.2 * logit * probs * (1.0 - probs)
+    )
+    rott[...] = base / clips_all
+    cgt[...] = 0.05 * slope / clips_all
     for k in range(3):
         wt[k * width : (k + 1) * width, :] = w[k * width : (k + 1) * width, :].T
     for copy in sent:
@@ -231,14 +244,9 @@
     stat2[0] = total
     sent = [send(stat2.at[0], stat2.at[r], T_LINE + r, line_peer(r)) for r in range(1, LINE)]
 
-    def turn(clip, carry):
-        base = pl.multiple_of(clip * clip_rows, clip_rows)
-        for frame in range(frames):
-            here = pl.ds(pl.multiple_of(base + frame * sites, sites), sites)
-            xt[:, here] = xs[here, :].T
-        return carry
-
-    lax.fori_loop(0, clips, turn, 0)
+    for frame in range(frames):
+        here = slice(frame * block, (frame + 1) * block)
+        xt[:, here] = xs[here, :].T
     for copy in sent:
         copy.wait()
     total = stat2[0]
@@ -261,67 +269,45 @@
     loss_ref[...] = total[bits : bits + 1, :] / tokens_all - 0.1 * code_entropy
     lean = jnp.log((1.0 - bit_mean) / bit_mean)
 
-    rotated = rott[...]
-    codes = jnp.tanh(rotated)
-    probs = (1.0 + codes) / 2.0
-    logit = 2.0 * rotated
-    slope = 1.0 - codes * codes
-    d_rot = (
-        cgt[...] * slope
-        + 0.5 * (rotated - codes) * (1.0 - slope)
-        - 0.2 * logit * probs * (1.0 - probs)
-        - 0.05 * slope * lean
-    ) / clips_all
-    d_lat = dot(rot, d_rot, NN, HIGHEST)
-    high = d_lat.astype(BF16)
-    dl[0:BITS_PAD, :] = high.astype(F32)
-    dl[BITS_PAD : 2 * BITS_PAD, :] = d_lat - high.astype(F32)
-
-    def back(clip, carry):
-        base = pl.multiple_of(clip * clip_rows, clip_rows)
-        for frame in range(frames):
-            here = pl.ds(pl.multiple_of(base + frame * sites, sites), sites)
-            a = dot(dl[:, here].T.astype(BF16), pp[...]) * gain
-            u = unit[here, :]
-            d_hidden = inv[here, :] * (a - u * jnp.mean(a * u, axis=1, keepdims=True))
-            dh[here, :] = d_hidden
-            dc[here, :] = d_hidden.astype(BF16)
-        return carry
-
-    lax.fori_loop(0, clips, back, 0)
+    d_lat = dot(rot, rott[...] - cgt[...] * lean, NN, HIGHEST)
+    high = d_lat.astype(BF16).astype(F32)
+    dl[0:BITS_PAD, :] = high
+    dl[BITS_PAD : 2 * BITS_PAD, :] = d_lat - high
+
+    for frame in range(frames):
+        here = slice(frame * block, (frame + 1) * block)
+        a = dot(dl[:, here].T.astype(BF16), pp[...]) * gain
+        u = unit[here, :]
+        d_hidden = inv[here, :] * (a - u * jnp.mean(a * u, axis=1, keepdims=True))
+        dc[here, :] = d_hidden.astype(BF16)
 
     core_peer = plane_peer(1)
     core_sent = []
     for k in range(3):
-        term = None
-        for clip in range(clips):
-            start = clip * clip_rows
-            depth = (frames - k) * sites
-            part = dot(
-                xt[:, start : start + depth],
-                dc[start + k * sites : start + clip_rows, :],
-            )
-            term = part if term is None else term + part
-        g[k * width : (k + 1) * width, :] = term
+        g[k * width : (k + 1) * width, :] = dot(xt[:, 0 : (frames - k) * block], dc[k * block :, :])
         for j in range(2):
             if (k + 1) * width >= (j + 1) * half > k * width:
                 rows = pl.ds(pl.multiple_of(j * half + (1 - c) * per_core, 8), per_core)
                 core_sent.append(send(g.at[rows], r1.at[j], T_CORE + j, core_peer))
 
-    def input_grad(clip):
-        base = clip * clip_rows
-        for frame in range(frames):
-            here = pl.ds(base + frame * sites, sites)
-            taps = min(frames - 1 - frame, 2) + 1
-            parts = [dc[pl.ds(base + (frame + k) * sites, sites), :] for k in range(taps)]
-            lhs = parts[0] if taps == 1 else jnp.concatenate(parts, axis=1)
-            ig[here, :] = (dh[here, :] + dot(lhs, wt[0 : taps * width, :])).astype(BF16)
-        rows = pl.ds(base, clip_rows)
-        copy = pltpu.make_async_copy(ig.at[rows], ig_hbm.at[rows], local_sem.at[IN_X + clips + clip])
-        copy.start()
-        return copy
-
     ig_out = []
+
+    def input_grad(frame):
+        here = slice(frame * block, (frame + 1) * block)
+        taps = min(frames - 1 - frame, 2) + 1
+        parts = [dc[(frame + k) * block : (frame + k + 1) * block, :] for k in range(taps)]
+        lhs = parts[0] if taps == 1 else jnp.concatenate(parts, axis=1)
+        ig[here, :] = (parts[0].astype(F32) + dot(lhs, wt[0 : taps * width, :])).astype(BF16)
+        for clip in range(clips):
+            copy = pltpu.make_async_copy(
+                ig.at[pl.ds(frame * block + clip * sites, sites)],
+                ig_hbm.at[pl.ds(clip * clip_rows + frame * sites, sites)],
+                local_sem.at[IN_X + (frames + frame) * clips + clip],
+            )
+            copy.start()
+            ig_out.append(copy)
+
+    input_grad(0)
     for copy in core_sent:
         copy.wait()
 
@@ -332,21 +318,22 @@
         rows = pl.ds(pl.multiple_of(side * half + c * per_core + x * per_x, 8), per_x)
         return g[rows, :] + r1[side, pl.ds(pl.multiple_of(x * per_x, 8), per_x), :]
 
+    kept = (1 - c) * s + c * h
     first_sent = []
-    for j in range(2):
+    for i, j in enumerate((1 - kept, kept)):
         s2[j] = summed((1 - c) * j + c * (1 - s), (1 - c) * (1 - h) + c * j).astype(BF16)
-        first_sent.append(send(s2.at[j], r2.at[j], T_FIRST + j, first_peer))
+        first_sent.append(send(s2.at[j], r2.at[j], T_FIRST + i, first_peer))
     for j in range(2):
         keep[j] = summed((1 - c) * j + c * s, (1 - c) * h + c * j)
-    ig_out.append(input_grad(0))
-    for copy in first_sent:
-        copy.wait()
-    kept = (1 - c) * s + c * h
+    input_grad(1)
+    first_sent[0].wait()
     s3[...] = (keep[1 - kept] + r2[1 - kept].astype(F32)).astype(BF16)
     second_sent = send(s3, r3, T_SECOND, second_peer)
-    keep[kept] = keep[kept] + r2[kept].astype(F32)
+    input_grad(2)
     m1_in.wait()
     m2_in.wait()
+    first_sent[1].wait()
+    keep[kept] = keep[kept] + r2[kept].astype(F32)
     second_sent.wait()
     mine = keep[kept] + r3[...].astype(F32)
     s4[...] = mine.astype(BF16)
@@ -355,8 +342,8 @@
     for r in range(1, LINE):
         rows = pl.ds(pl.multiple_of(line_at(r) * own, 16), own)
         rows_sent.append(send(s4.at[rows], r4.at[r], T_ROWS + r, line_peer(r)))
-    for clip in range(1, clips):
-        ig_out.append(input_grad(clip))
+    for frame in range(3, frames):
+        input_grad(frame)
     for copy in rows_sent:
         copy.wait()
     grad = keep[kept, pl.ds(pl.multiple_of(z * own, 8), own), :]
@@ -374,18 +361,12 @@
         for r in range(1, far_size):
             grad = grad + far[r]
 
-    mine_at = c * per_core + h * per_x
-    own_rows = pl.ds(pl.multiple_of(mine_at + z * own, 16), own)
-    gr[own_rows, :] = grad.astype(BF16)
-    sent = [
-        send(gr.at[own_rows], gr.at[own_rows], T_GATHER + r, line_peer(r)) for r in range(1, LINE)
-    ]
-    for copy in sent:
-        copy.wait()
+    def chunk(core, x, r):
+        return core * per_core + x * per_x + line_at(r) * own
 
     def update(at):
-        rows = pl.ds(pl.multiple_of(at, 16), per_x)
-        here = pl.ds(pl.multiple_of(s * half + at, 16), per_x)
+        rows = pl.ds(pl.multiple_of(at, 16), own)
+        here = pl.ds(pl.multiple_of(s * half + at, 16), own)
         value = gr[rows, :].astype(F32)
         first = 0.9 * m1[rows, :] + 0.1 * value
         second = 0.99 * m2[rows, :] + 0.01 * value * value
@@ -394,34 +375,57 @@
         stepped = w[here, :].astype(F32) - 0.001 * first / (jnp.sqrt(second) + 1e-08)
         nw[here, :] = stepped.astype(BF16)
 
-    def grad_rows(at):
-        return gr.at[pl.ds(pl.multiple_of(at, 16), per_x)]
-
-    def new_rows(side, at):
-        return nw.at[pl.ds(pl.multiple_of(side * half + at, 16), per_x)]
+    def send_grad(at, index, peer):
+        rows = gr.at[pl.ds(pl.multiple_of(at, 16), own)]
+        return send(rows, rows, index, peer)
+
+    def send_new(side, at, index, peer):
+        rows = nw.at[pl.ds(pl.multiple_of(side * half + at, 16), own)]
+        return send(rows, rows, index, peer)
 
     x_peer, y_peer = plane_peer(2), plane_peer(4)
-    other_at = c * per_core + (1 - h) * per_x
-    grad_x = send(grad_rows(mine_at), grad_rows(mine_at), T_GRAD_X, x_peer)
-    grad_core = [send(grad_rows(mine_at), grad_rows(mine_at), T_GRAD_CORE, core_peer)]
-    update(mine_at)
-    new_y = [send(new_rows(s, mine_at), new_rows(s, mine_at), T_NEW_Y, y_peer)]
-    grad_x.wait()
-    grad_core.append(send(grad_rows(other_at), grad_rows(other_at), T_GRAD_CORE + 1, core_peer))
-    update(other_at)
-    new_y.append(send(new_rows(s, other_at), new_rows(s, other_at), T_NEW_Y + 1, y_peer))
-    grad_core[0].wait()
-    update((1 - c) * per_core + h * per_x)
-    grad_core[1].wait()
-    update((1 - c) * per_core + (1 - h) * per_x)
+    own_at = chunk(c, h, 0)
+    gr[pl.ds(pl.multiple_of(own_at, 16), own), :] = grad.astype(BF16)
+    gather = [send_grad(own_at, T_GATHER + r, line_peer(r)) for r in range(1, LINE)]
+    grad_x, grad_core, new_y, new_x, new_core = [], [], [], [], []
+    for r in range(LINE):
+        at = chunk(c, h, r)
+        if r > 0:
+            gather[r - 1].wait()
+        grad_x.append(send_grad(at, T_GRAD_X + r, x_peer))
+        update(at)
+        new_y.append(send_new(s, at, T_NEW_Y + r, y_peer))
+        grad_core.append(send_grad(at, T_GRAD_CORE + r, core_peer))
+    for r in range(2):
+        at = chunk(c, h, r)
+        new_y[r].wait()
+        new_x.append(send_new(1 - s, at, T_NEW_X + r, x_peer))
+        new_core.append(send_new(1 - s, at, T_NEW_CORE + r, core_peer))
+    for r in (2, 3, 0, 1):
+        at = chunk(c, 1 - h, r)
+        grad_x[r].wait()
+        update(at)
+        if r >= 2:
+            new_y.append(send_new(s, at, T_NEW_Y + 2 + r, y_peer))
+        grad_core.append(send_grad(at, T_GRAD_CORE + 4 + r, core_peer))
+    for r in range(2, 4):
+        new_y[r].wait()
+        new_core.append(send_new(1 - s, chunk(c, h, r), T_NEW_CORE + r, core_peer))
+    for copy in grad_core:
+        copy.wait()
+    for r in range(LINE):
+        update(chunk(1 - c, h, r))
+        update(chunk(1 - c, 1 - h, r))
     m1_out = pltpu.make_async_copy(m1, m1o_hbm, local_sem.at[OUT_M1])
     m1_out.start()
     m2_out = pltpu.make_async_copy(m2, m2o_hbm, local_sem.at[OUT_M2])
     m2_out.start()
-    new_core = []
-    for j, at in enumerate((mine_at, other_at)):
-        new_y[j].wait()
-        new_core.append(send(new_rows(1 - s, at), new_rows(1 - s, at), T_NEW_CORE + j, core_peer))
+    for r in range(2):
+        new_x[r].wait()
+        new_core.append(send_new(1 - s, chunk(c, 1 - h, r), T_NEW_CORE + 4 + r, core_peer))
+    for r in range(2, 4):
+        new_y[2 + r].wait()
+        new_core.append(send_new(1 - s, chunk(c, 1 - h, r), T_NEW_CORE + 4 + r, core_peer))
     for copy in new_core:
         copy.wait()
     nw_out = pltpu.make_async_copy(nw, nw_hbm, local_sem.at[OUT_W])
@@ -431,6 +435,20 @@
     m1_out.wait()
     m2_out.wait()
     nw_out.wait()
+
+
+def hand_over(*refs):
+    sources, targets, sem = refs[:4], refs[4:8], refs[8]
+    copies = []
+    for i, (source, target) in enumerate(zip(sources, targets)):
+        step = source.shape[0] // PIECES
+        for j in range(PIECES):
+            rows = pl.ds(j * step, step)
+            copy = pltpu.make_async_copy(source.at[rows], target.at[rows], sem.at[i * PIECES + j])
+            copy.start()
+            copies.append(copy)
+    for copy in copies:
+        copy.wait()
 
 
 def on_device(
@@ -469,14 +487,14 @@
         vmem((width, tokens), BF16),
         vmem((rows, width), BF16),
         vmem((rows, width), BF16),
-        vmem((tokens, bits), BF16),
+        vmem((frames, bits, count, sites), BF16),
         vmem((tokens, width), F32),
         vmem((tokens, 1), F32),
         vmem((BITS_PAD, tokens), F32),
         vmem((BITS_PAD, tokens), F32),
+        vmem((BITS_PAD, tokens), F32),
         vmem((128, tokens), F32),
         vmem((128, width), BF16),
-        vmem((tokens, width), F32),
         vmem((tokens, width), BF16),
         vmem((tokens, width), BF16),
         vmem((half, width), F32),
@@ -496,13 +514,13 @@
         vmem((PLANE, BITS_PAD, 128), F32),
         vmem((LINE, BITS_PAD, 128), F32),
         vmem((far_size, BITS_PAD, 128), F32),
-        pltpu.SemaphoreType.DMA((IN_X + 2 * count,)),
+        pltpu.SemaphoreType.DMA((IN_X + 2 * count * frames,)),
         pltpu.SemaphoreType.DMA((T_FAR + 2 * far_size,)),
         pltpu.SemaphoreType.DMA((T_FAR + 2 * far_size,)),
     ]
     whole = pl.BlockSpec(memory_space=pltpu.VMEM)
     outside = pl.BlockSpec(memory_space=pl.ANY)
-    new_weight, first_out, second_out, input_grad, loss = pl.pallas_call(
+    *large, loss = pl.pallas_call(
         functools.partial(kernel, sizes),
         out_shape=(
             jax.ShapeDtypeStruct((rows, width), BF16),
@@ -515,19 +533,27 @@
         out_specs=(outside, outside, outside, outside, whole),
         scratch_shapes=scratch,
         compiler_params=pltpu.CompilerParams(
-            collective_id=0, has_side_effects=True, vmem_limit_bytes=60 * 1024 * 1024
+            collective_id=0, has_side_effects=True, vmem_limit_bytes=VMEM_BYTES
         ),
     )(
         clips.reshape(tokens, width),
-        code_grad.reshape(tokens, bits),
+        code_grad.transpose(1, 3, 0, 2),
         conv_weight,
         norm_gain.reshape(1, width),
-        proj_weight,
+        proj_weight.T,
         code_bias.reshape(1, bits),
         rotation,
         first_moment,
         second_moment,
     )
+    new_weight, first_out, second_out, input_grad = pl.pallas_call(
+        hand_over,
+        out_shape=tuple(jax.ShapeDtypeStruct(a.shape, a.dtype) for a in large),
+        in_specs=[outside] * 4,
+        out_specs=(outside,) * 4,
+        scratch_shapes=[pltpu.SemaphoreType.DMA((4 * PIECES,))],
+        compiler_params=pltpu.CompilerParams(vmem_limit_bytes=VMEM_BYTES),
+    )(*large)
     return (
         new_weight,
         first_out,

time: 82.2 us -> 288 us (3.50)
  Pallas kernels: 67.3 us -> 285 us
  local copies, waits for them, and re-layouts: 12.1 us -> 0 us
    pallas_call x0 -> x1, Pallas kernels: none -> 224 us  [on_device(): pl.pallas_call(hand_over, out_shape=tuple((jax.ShapeDtypeStruct(a.shape,...]
    unnamed x12 -> x0, local copies, waits for them, and re-layouts: 12.1 us -> none
    pallas_call x1, Pallas kernels: 67.3 us -> 61.5 us  [on_device(): pl.pallas_call(functools.partial(kernel, sizes), out_shape=(jax.ShapeDtyp...]
where the time goes in v2:
time: 288 us; the launch traced here: 287 us
  Pallas kernels  285 us (99%)
    pallas_call x1, Pallas kernels, on_device(): pl.pallas_call(hand_over, out_shape=tuple((jax.ShapeDtypeStruct(a.shape,...  224 us
    pallas_call x1, Pallas kernels, on_device(): pl.pallas_call(functools.partial(kernel, sizes), out_shape=(jax.ShapeDtyp...  61.5 us

profile of v2, /device:TPU:0, one launch (start us, length us, event | category | flops | bytes accessed | tf_op | source)
XLA Modules:
  0.0 287.4 jit_solution(16847385235316926140)
XLA Ops:
  0.6 61.5 %shard_map.128 = (bf16[1536,512]{1,0:T(8,128)(2,1)}, f32[768,512]{1,0:T(8,128)}, f32[768,512]{1,0:T(8,128)}, bf16[2560,512]{1,0:T(8,128)(2,1)}, f32[1,1]{1,0:T(1,128)}) custom-call(bf16[2560,512]{1,0:T(8,128)(2,1)} %bitcast.7, bf16[5,18,2,256]{3,2,1,0:T(2,128)(2,1)} %bitcast.8, bf16[1536,512]{1,0:T(8,128)(2,1)} %weight_hbm.1, f32[1,512]{1,0:T(1,128)} %bitcast.10, ...), custom_call_target="tpu_custom_call" | custom-call | tf_op jit(solution)/shard_map/pallas_call | solution.py:523
  62.2 223.5 %shard_map.129 = (bf16[1536,512]{1,0:T(8,128)(2,1)}, f32[768,512]{1,0:T(8,128)}, f32[768,512]{1,0:T(8,128)}, bf16[2560,512]{1,0:T(8,128)(2,1)}) custom-call(bf16[1536,512]{1,0:T(8,128)(2,1)} %get-tuple-element.14.refs_0_, f32[768,512]{1,0:T(8,128)} %get-tuple-element.15.refs_1_, f32[768,512]{1,0:T(8,128)} %get-tuple-element.16.refs_2_, ...), custom_call_target="tpu_custom_call" | custom-call | tf_op jit(solution)/shard_map/pallas_call | solution.py:549

commit v3 on v2

--- a/solution.py
+++ b/solution.py
@@ -15,7 +15,7 @@
 PLANE = 8
 LINE = 4
 DEPTH = 16
-PIECES = 2
+PIECES = 4
 VMEM_BYTES = 60 * 1024 * 1024
 
 IN_W, IN_CG, IN_M1, IN_M2, OUT_W, OUT_M1, OUT_M2, IN_X = range(8)
@@ -70,7 +70,6 @@
     cg,
     unit,
     inv,
-    lat,
     rott,
     cgt,
     dl,
@@ -171,15 +170,18 @@
     )
     eye = jnp.where(eye_mask, 1.0, 0.0).astype(F32)
     eye16 = eye.astype(BF16)
-    proj_t = dot(eye16, proj_ref[...]).astype(BF16)
+    rot_rows = dot(eye, rot_ref[...], NN, HIGHEST)
+    rot_t = dot(eye, rot_rows, NT, HIGHEST)
+    proj_t = dot(rot_t, dot(eye16, proj_ref[...]), NN, HIGHEST)
+    proj_high = proj_t.astype(BF16)
+    proj_low = (proj_t - proj_high.astype(F32)).astype(BF16)
     pp[...] = jnp.zeros_like(pp)
-    pp[0:BITS_PAD, :] = proj_t
-    pp[BITS_PAD : 2 * BITS_PAD, :] = proj_t
+    pp[0:BITS_PAD, :] = proj_high
+    pp[BITS_PAD : 2 * BITS_PAD, :] = proj_low
+    pp[2 * BITS_PAD : 3 * BITS_PAD, :] = proj_high
     dl[...] = jnp.zeros_like(dl)
-    rot_rows = dot(eye, rot_ref[...], NN, HIGHEST)
-    rot = dot(rot_rows, eye, NT, HIGHEST)
-    rot_t = dot(eye, rot_rows, NT, HIGHEST)
     bias = jnp.sum(jnp.where(eye_mask, bias_ref[...], 0.0), axis=1, keepdims=True)
+    bias = dot(rot_t, jnp.broadcast_to(bias, (BITS_PAD, 128)), NN, HIGHEST)[:, 0:1]
     gain = gain_ref[...]
 
     w_in.wait()
@@ -197,9 +199,10 @@
         unit[here, :] = u
         inv[here, :] = scale
         normed = (u * gain).astype(BF16)
-        lat[:, here] = dot(proj_t, normed, NT) + bias
-
-    rott[...] = dot(rot_t, lat[...], NN, HIGHEST)
+        both = dot(pp[0 : 2 * BITS_PAD, :], normed, NT)
+        rott[:, here] = both[0:BITS_PAD, :] + both[BITS_PAD:, :] + bias
+        xt[:, here] = xs[here, :].T
+
     cg_in.wait()
     cgt[...] = jnp.zeros_like(cgt)
     for frame in range(frames):
@@ -244,9 +247,6 @@
     stat2[0] = total
     sent = [send(stat2.at[0], stat2.at[r], T_LINE + r, line_peer(r)) for r in range(1, LINE)]
 
-    for frame in range(frames):
-        here = slice(frame * block, (frame + 1) * block)
-        xt[:, here] = xs[here, :].T
     for copy in sent:
         copy.wait()
     total = stat2[0]
@@ -269,10 +269,11 @@
     loss_ref[...] = total[bits : bits + 1, :] / tokens_all - 0.1 * code_entropy
     lean = jnp.log((1.0 - bit_mean) / bit_mean)
 
-    d_lat = dot(rot, rott[...] - cgt[...] * lean, NN, HIGHEST)
-    high = d_lat.astype(BF16).astype(F32)
+    d_rot = rott[...] - cgt[...] * lean
+    high = d_rot.astype(BF16).astype(F32)
     dl[0:BITS_PAD, :] = high
-    dl[BITS_PAD : 2 * BITS_PAD, :] = d_lat - high
+    dl[BITS_PAD : 2 * BITS_PAD, :] = high
+    dl[2 * BITS_PAD : 3 * BITS_PAD, :] = d_rot - high
 
     for frame in range(frames):
         here = slice(frame * block, (frame + 1) * block)
@@ -438,17 +439,23 @@
 
 
 def hand_over(*refs):
-    sources, targets, sem = refs[:4], refs[4:8], refs[8]
-    copies = []
-    for i, (source, target) in enumerate(zip(sources, targets)):
+    sources, targets, stages, in_sem, out_sem = refs[:4], refs[4:8], refs[8:12], refs[12], refs[13]
+    loads, stores = [], []
+    for i, (source, stage) in enumerate(zip(sources, stages)):
         step = source.shape[0] // PIECES
         for j in range(PIECES):
             rows = pl.ds(j * step, step)
-            copy = pltpu.make_async_copy(source.at[rows], target.at[rows], sem.at[i * PIECES + j])
-            copy.start()
-            copies.append(copy)
-    for copy in copies:
-        copy.wait()
+            index = i * PIECES + j
+            load = pltpu.make_async_copy(source.at[rows], stage.at[rows], in_sem.at[index])
+            load.start()
+            loads.append(load)
+            store = pltpu.make_async_copy(stage.at[rows], targets[i].at[rows], out_sem.at[index])
+            stores.append(store)
+    for load, store in zip(loads, stores):
+        load.wait()
+        store.start()
+    for store in stores:
+        store.wait()
 
 
 def on_device(
@@ -490,7 +497,6 @@
         vmem((frames, bits, count, sites), BF16),
         vmem((tokens, width), F32),
         vmem((tokens, 1), F32),
-        vmem((BITS_PAD, tokens), F32),
         vmem((BITS_PAD, tokens), F32),
         vmem((BITS_PAD, tokens), F32),
         vmem((128, tokens), F32),
@@ -551,7 +557,8 @@
         out_shape=tuple(jax.ShapeDtypeStruct(a.shape, a.dtype) for a in large),
         in_specs=[outside] * 4,
         out_specs=(outside,) * 4,
-        scratch_shapes=[pltpu.SemaphoreType.DMA((4 * PIECES,))],
+        scratch_shapes=[vmem(a.shape, a.dtype) for a in large]
+        + [pltpu.SemaphoreType.DMA((4 * PIECES,))] * 2,
         compiler_params=pltpu.CompilerParams(vmem_limit_bytes=VMEM_BYTES),
     )(*large)
     return (

time: 288 us -> 69.7 us (0.24)
  Pallas kernels: 285 us -> 67.1 us
    pallas_call x1, Pallas kernels: 224 us -> 5.9 us  [on_device(): pl.pallas_call(hand_over, out_shape=tuple((jax.ShapeDtypeStruct(a.shape,...]
where the time goes in v3:
time: 69.7 us; the launch traced here: 69.5 us
  Pallas kernels  67.1 us (96%)
  between operations  2.38 us (3%)
    pallas_call x1, Pallas kernels, on_device(): pl.pallas_call(functools.partial(kernel, sizes), out_shape=(jax.ShapeDtyp...  61.2 us
    pallas_call x1, Pallas kernels, on_device(): pl.pallas_call(hand_over, out_shape=tuple((jax.ShapeDtypeStruct(a.shape,...  5.9 us

profile of v3, /device:TPU:0, one launch (start us, length us, event | category | flops | bytes accessed | tf_op | source)
XLA Modules:
  0.0 69.5 jit_solution(1065192320965200559)
XLA Ops:
  0.6 61.2 %shard_map.128 = (bf16[1536,512]{1,0:T(8,128)(2,1)}, f32[768,512]{1,0:T(8,128)}, f32[768,512]{1,0:T(8,128)}, bf16[2560,512]{1,0:T(8,128)(2,1)}, f32[1,1]{1,0:T(1,128)}) custom-call(bf16[2560,512]{1,0:T(8,128)(2,1)} %bitcast.7, bf16[5,18,2,256]{3,2,1,0:T(2,128)(2,1)} %bitcast.8, bf16[1536,512]{1,0:T(8,128)(2,1)} %weight_hbm.1, f32[1,512]{1,0:T(1,128)} %bitcast.10, ...), custom_call_target="tpu_custom_call" | custom-call | tf_op jit(solution)/shard_map/pallas_call | solution.py:529
  61.8 5.9 %shard_map.129 = (bf16[1536,512]{1,0:T(8,128)(2,1)}, f32[768,512]{1,0:T(8,128)}, f32[768,512]{1,0:T(8,128)}, bf16[2560,512]{1,0:T(8,128)(2,1)}) custom-call(bf16[1536,512]{1,0:T(8,128)(2,1)} %get-tuple-element.14.refs_0_, f32[768,512]{1,0:T(8,128)} %get-tuple-element.15.refs_1_, f32[768,512]{1,0:T(8,128)} %get-tuple-element.16.refs_2_, ...), custom_call_target="tpu_custom_call" | custom-call | tf_op jit(solution)/shard_map/pallas_call | solution.py:555

commit v4 on v3

--- a/solution.py
+++ b/solution.py
@@ -79,6 +79,7 @@
     m1,
     m2,
     g,
+    gs,
     r1,
     keep,
     s2,
@@ -101,8 +102,9 @@
     clip_rows = frames * sites
     block = clips * sites
     half = m1.shape[0]
-    per_core, per_x = half // 2, half // 4
-    own = half // DEPTH
+    per_x = half // 2
+    own = per_x // LINE
+    cols = width // 2
     dp = lax.axis_index("dp")
     s = lax.axis_index("shard")
     c = dp % 2
@@ -284,12 +286,21 @@
 
     core_peer = plane_peer(1)
     core_sent = []
+
+    def columns(core):
+        return pl.ds(pl.multiple_of(core * cols, cols), cols)
+
+    def term(k, core):
+        return dot(xt[:, 0 : (frames - k) * block], dc[k * block :, columns(core)])
+
     for k in range(3):
-        g[k * width : (k + 1) * width, :] = dot(xt[:, 0 : (frames - k) * block], dc[k * block :, :])
+        gs[k * width : (k + 1) * width, :] = term(k, 1 - c).astype(BF16)
         for j in range(2):
             if (k + 1) * width >= (j + 1) * half > k * width:
-                rows = pl.ds(pl.multiple_of(j * half + (1 - c) * per_core, 8), per_core)
-                core_sent.append(send(g.at[rows], r1.at[j], T_CORE + j, core_peer))
+                rows = slice(j * half, (j + 1) * half)
+                core_sent.append(send(gs.at[rows], r1.at[rows], T_CORE + j, core_peer))
+    for k in range(3):
+        g[k * width : (k + 1) * width, :] = term(k, c)
 
     ig_out = []
 
@@ -308,7 +319,6 @@
             copy.start()
             ig_out.append(copy)
 
-    input_grad(0)
     for copy in core_sent:
         copy.wait()
 
@@ -316,8 +326,8 @@
     second_peer = (dp + c * 2 * (1 - 2 * h), s + (1 - c) * (1 - 2 * s))
 
     def summed(side, x):
-        rows = pl.ds(pl.multiple_of(side * half + c * per_core + x * per_x, 8), per_x)
-        return g[rows, :] + r1[side, pl.ds(pl.multiple_of(x * per_x, 8), per_x), :]
+        rows = pl.ds(pl.multiple_of(side * half + x * per_x, 16), per_x)
+        return g[rows, :] + r1[rows, :].astype(F32)
 
     kept = (1 - c) * s + c * h
     first_sent = []
@@ -326,6 +336,7 @@
         first_sent.append(send(s2.at[j], r2.at[j], T_FIRST + i, first_peer))
     for j in range(2):
         keep[j] = summed((1 - c) * j + c * s, (1 - c) * h + c * j)
+    input_grad(0)
     input_grad(1)
     first_sent[0].wait()
     s3[...] = (keep[1 - kept] + r2[1 - kept].astype(F32)).astype(BF16)
@@ -362,80 +373,85 @@
         for r in range(1, far_size):
             grad = grad + far[r]
 
-    def chunk(core, x, r):
-        return core * per_core + x * per_x + line_at(r) * own
-
-    def update(at):
+    def chunk(x, r):
+        return x * per_x + line_at(r) * own
+
+    def update(core, at):
         rows = pl.ds(pl.multiple_of(at, 16), own)
         here = pl.ds(pl.multiple_of(s * half + at, 16), own)
-        value = gr[rows, :].astype(F32)
-        first = 0.9 * m1[rows, :] + 0.1 * value
-        second = 0.99 * m2[rows, :] + 0.01 * value * value
-        m1[rows, :] = first
-        m2[rows, :] = second
-        stepped = w[here, :].astype(F32) - 0.001 * first / (jnp.sqrt(second) + 1e-08)
-        nw[here, :] = stepped.astype(BF16)
+        value = gr[core, rows, :].astype(F32)
+        first = 0.9 * m1[rows, columns(core)] + 0.1 * value
+        second = 0.99 * m2[rows, columns(core)] + 0.01 * value * value
+        m1[rows, columns(core)] = first
+        m2[rows, columns(core)] = second
+        stepped = w[here, columns(core)].astype(F32) - 0.001 * first / (jnp.sqrt(second) + 1e-08)
+        nw[core, here, :] = stepped.astype(BF16)
 
     def send_grad(at, index, peer):
-        rows = gr.at[pl.ds(pl.multiple_of(at, 16), own)]
+        rows = gr.at[c, pl.ds(pl.multiple_of(at, 16), own)]
         return send(rows, rows, index, peer)
 
     def send_new(side, at, index, peer):
-        rows = nw.at[pl.ds(pl.multiple_of(side * half + at, 16), own)]
+        rows = nw.at[c, pl.ds(pl.multiple_of(side * half + at, 16), own)]
         return send(rows, rows, index, peer)
 
     x_peer, y_peer = plane_peer(2), plane_peer(4)
-    own_at = chunk(c, h, 0)
-    gr[pl.ds(pl.multiple_of(own_at, 16), own), :] = grad.astype(BF16)
+    own_at = chunk(h, 0)
+    gr[c, pl.ds(pl.multiple_of(own_at, 16), own), :] = grad.astype(BF16)
     gather = [send_grad(own_at, T_GATHER + r, line_peer(r)) for r in range(1, LINE)]
     grad_x, grad_core, new_y, new_x, new_core = [], [], [], [], []
     for r in range(LINE):
-        at = chunk(c, h, r)
+        at = chunk(h, r)
         if r > 0:
             gather[r - 1].wait()
         grad_x.append(send_grad(at, T_GRAD_X + r, x_peer))
-        update(at)
+        update(c, at)
         new_y.append(send_new(s, at, T_NEW_Y + r, y_peer))
         grad_core.append(send_grad(at, T_GRAD_CORE + r, core_peer))
     for r in range(2):
-        at = chunk(c, h, r)
+        at = chunk(h, r)
         new_y[r].wait()
         new_x.append(send_new(1 - s, at, T_NEW_X + r, x_peer))
         new_core.append(send_new(1 - s, at, T_NEW_CORE + r, core_peer))
     for r in (2, 3, 0, 1):
-        at = chunk(c, 1 - h, r)
+        at = chunk(1 - h, r)
         grad_x[r].wait()
-        update(at)
+        update(c, at)
         if r >= 2:
             new_y.append(send_new(s, at, T_NEW_Y + 2 + r, y_peer))
         grad_core.append(send_grad(at, T_GRAD_CORE + 4 + r, core_peer))
     for r in range(2, 4):
         new_y[r].wait()
-        new_core.append(send_new(1 - s, chunk(c, h, r), T_NEW_CORE + r, core_peer))
+        new_core.append(send_new(1 - s, chunk(h, r), T_NEW_CORE + r, core_peer))
     for copy in grad_core:
         copy.wait()
     for r in range(LINE):
-        update(chunk(1 - c, h, r))
-        update(chunk(1 - c, 1 - h, r))
+        update(1 - c, chunk(h, r))
+        update(1 - c, chunk(1 - h, r))
     m1_out = pltpu.make_async_copy(m1, m1o_hbm, local_sem.at[OUT_M1])
     m1_out.start()
     m2_out = pltpu.make_async_copy(m2, m2o_hbm, local_sem.at[OUT_M2])
     m2_out.start()
     for r in range(2):
         new_x[r].wait()
-        new_core.append(send_new(1 - s, chunk(c, 1 - h, r), T_NEW_CORE + 4 + r, core_peer))
+        new_core.append(send_new(1 - s, chunk(1 - h, r), T_NEW_CORE + 4 + r, core_peer))
     for r in range(2, 4):
         new_y[2 + r].wait()
-        new_core.append(send_new(1 - s, chunk(c, 1 - h, r), T_NEW_CORE + 4 + r, core_peer))
+        new_core.append(send_new(1 - s, chunk(1 - h, r), T_NEW_CORE + 4 + r, core_peer))
     for copy in new_core:
         copy.wait()
-    nw_out = pltpu.make_async_copy(nw, nw_hbm, local_sem.at[OUT_W])
-    nw_out.start()
+    nw_out = []
+    for core in range(2):
+        target = nw_hbm.at[:, core * cols : (core + 1) * cols]
+        copy = pltpu.make_async_copy(nw.at[core], target, local_sem.at[(OUT_W, IN_W)[core]])
+        copy.start()
+        nw_out.append(copy)
     for copy in ig_out:
         copy.wait()
     m1_out.wait()
     m2_out.wait()
-    nw_out.wait()
+    for copy in nw_out:
+        copy.wait()
 
 
 def hand_over(*refs):
@@ -476,7 +492,8 @@
     far_size = dp_size // DEPTH
     tokens = count * frames * sites
     rows, half = conv_weight.shape[0], first_moment.shape[0]
-    per_core, per_x, own = half // 2, half // 4, half // DEPTH
+    per_x, cols = half // 2, width // 2
+    own = per_x // LINE
     sizes = (
         count,
         frames,
@@ -505,18 +522,19 @@
         vmem((tokens, width), BF16),
         vmem((half, width), F32),
         vmem((half, width), F32),
-        vmem((rows, width), F32),
-        vmem((2, per_core, width), F32),
-        vmem((2, per_x, width), F32),
-        vmem((2, per_x, width), BF16),
-        vmem((2, per_x, width), BF16),
-        vmem((per_x, width), BF16),
-        vmem((per_x, width), BF16),
-        vmem((per_x, width), BF16),
-        vmem((LINE, own, width), BF16),
-        vmem((far_size, own, width), F32),
-        vmem((half, width), BF16),
-        vmem((rows, width), BF16),
+        vmem((rows, cols), F32),
+        vmem((rows, cols), BF16),
+        vmem((rows, cols), BF16),
+        vmem((2, per_x, cols), F32),
+        vmem((2, per_x, cols), BF16),
+        vmem((2, per_x, cols), BF16),
+        vmem((per_x, cols), BF16),
+        vmem((per_x, cols), BF16),
+        vmem((per_x, cols), BF16),
+        vmem((LINE, own, cols), BF16),
+        vmem((far_size, own, cols), F32),
+        vmem((2, half, cols), BF16),
+        vmem((2, rows, cols), BF16),
         vmem((PLANE, BITS_PAD, 128), F32),
         vmem((LINE, BITS_PAD, 128), F32),
         vmem((far_size, BITS_PAD, 128), F32),

time: 69.7 us -> 66.3 us (0.951)
  Pallas kernels: 67.1 us -> 63.7 us
    pallas_call x1, Pallas kernels: 61.2 us -> 57.8 us  [on_device(): pl.pallas_call(functools.partial(kernel, sizes), out_shape=(jax.ShapeDtyp...]
where the time goes in v4:
time: 66.3 us; the launch traced here: 66.1 us
  Pallas kernels  63.7 us (96%)
  between operations  2.38 us (4%)
    pallas_call x1, Pallas kernels, on_device(): pl.pallas_call(functools.partial(kernel, sizes), out_shape=(jax.ShapeDtyp...  57.8 us
    pallas_call x1, Pallas kernels, on_device(): pl.pallas_call(hand_over, out_shape=tuple((jax.ShapeDtypeStruct(a.shape,...  5.9 us

profile of v4, /device:TPU:0, one launch (start us, length us, event | category | flops | bytes accessed | tf_op | source)
XLA Modules:
  0.0 66.1 jit_solution(7621173117673337900)
XLA Ops:
  0.6 57.8 %shard_map.128 = (bf16[1536,512]{1,0:T(8,128)(2,1)}, f32[768,512]{1,0:T(8,128)}, f32[768,512]{1,0:T(8,128)}, bf16[2560,512]{1,0:T(8,128)(2,1)}, f32[1,1]{1,0:T(1,128)}) custom-call(bf16[2560,512]{1,0:T(8,128)(2,1)} %bitcast.7, bf16[5,18,2,256]{3,2,1,0:T(2,128)(2,1)} %bitcast.8, bf16[1536,512]{1,0:T(8,128)(2,1)} %weight_hbm.1, f32[1,512]{1,0:T(1,128)} %bitcast.10, ...), custom_call_target="tpu_custom_call" | custom-call | tf_op jit(solution)/shard_map/pallas_call | solution.py:547
  58.4 5.9 %shard_map.129 = (bf16[1536,512]{1,0:T(8,128)(2,1)}, f32[768,512]{1,0:T(8,128)}, f32[768,512]{1,0:T(8,128)}, bf16[2560,512]{1,0:T(8,128)(2,1)}) custom-call(bf16[1536,512]{1,0:T(8,128)(2,1)} %get-tuple-element.14.refs_0_, f32[768,512]{1,0:T(8,128)} %get-tuple-element.15.refs_1_, f32[768,512]{1,0:T(8,128)} %get-tuple-element.16.refs_2_, ...), custom_call_target="tpu_custom_call" | custom-call | tf_op jit(solution)/shard_map/pallas_call | solution.py:573
